TPU v7x, 768 devices: a whole 4x8x12 slice. The times are simulated.
768 devices in a mesh: row: 16 (over x, y_hi), col: 48 (over z, y_lo, core).
Axes of the slice: x: 4, y: 8 (y_hi: 4, y_lo: 2; y = y_hi * 2 + y_lo), z: 12, core: 2. Of those that a mesh axis runs over, the one named last changes fastest.
Arguments:
- p_blocks: bfloat16 [64, 48, 128, 128], P('row', 'col'), may hold values from -0.29882812 to 0.29882812
- p_cols: int32 [64, 48], P('row', 'col'), may hold values from -1 to 767, as said below
- h_blocks: bfloat16 [32, 96, 128, 128], P('row', 'col'), may hold values from -3 to 3
- h_rows: int32 [32, 96], P('row', 'col'), may hold values from -1 to 767, as said below
- keep: int32 [64, 96], P('row', 'col'), may hold values 0 or 1
Outputs:
- product: bfloat16 [64, 96, 128, 128], P('row', 'col')
Inputs may be any that keep to these rules, and one draw needn't show every extreme that they name: `p_cols`: entry (i, c) is -1 or a block column from c * 16 to c * 16 + 15. `h_rows`: entry (t, j) is -1 or a block row from r * 48 to r * 48 + 47, where r = t // 2; the entries of one block column that are not -1 are distinct.
All inputs are finite; a program needn't handle non-finite values. No bound on the sum of `keep` on one device may be relied on, other than what follows from the above.
Results may differ from a plain program's by a relative error of at most 0.001.
Values may be sent and summed in bfloat16 or wider, within the bound.
A program may use at most 64 MiB of HBM per device.

v0:
```python
import jax
import jax.numpy as jnp
from jax import lax
from jax.sharding import PartitionSpec as P


def shards(p_blocks, p_cols, h_blocks, h_rows, keep):
    cols_here = h_blocks.shape[1]
    column_ids = jnp.arange(cols_here, dtype=jnp.int32)
    h_all, hrow_all = (
        lax.all_gather(h_blocks, "row", axis=0, tiled=True),
        lax.all_gather(h_rows, "row", axis=0, tiled=True),
    )
    dense_blocks = lax.all_gather(p_blocks, "col", axis=1, tiled=True)
    dense_cols = lax.all_gather(p_cols, "col", axis=1, tiled=True)
    matches = (dense_cols[:, :, None, None] == hrow_all[None, None]) & (dense_cols >= 0)[
        :, :, None, None
    ]
    slot_ids = lax.broadcasted_iota(jnp.int32, matches.shape, 2)
    target = jnp.sum(jnp.where(matches, slot_ids, 0), axis=2)
    has_slot = jnp.any(matches, axis=2)
    picked = h_all[target, column_ids[None, None, :]]
    picked = jnp.where(has_slot[..., None, None], picked, jnp.zeros((), picked.dtype))
    summed = jnp.einsum(
        "inab,injbc->ijac", dense_blocks, picked, preferred_element_type=jnp.float32
    )
    kept = jnp.where((keep == 1)[:, :, None, None], summed, jnp.zeros((), jnp.float32))
    return kept.astype(jnp.bfloat16)


def solution(mesh):
    return jax.shard_map(
        shards,
        mesh=mesh,
        in_specs=(
            P("row", "col", None, None),
            P("row", "col"),
            P("row", "col", None, None),
            P("row", "col"),
            P("row", "col"),
        ),
        out_specs=P("row", "col", None, None),
        check_vma=False,
    )
```

profile of v0, /device:TPU:1, one launch (start us, length us, event | category | flops | bytes accessed | tf_op | source)
XLA Modules:
  0.0 206.8 jit_solution(13450611225111995513)
XLA Ops:
  6.5 0.0 all-gather.5.cloned.1.call-start
  6.5 0.7 all-gather.5.cloned.1.call-update
  7.3 0.0 all-gather.7.cloned.1.call-start
  7.3 0.7 all-gather.7.cloned.1.call-update
  8.0 59.7 %all-gather = s32[48,1,4]{2,1,0:T(1,128)S(1)} all-gather(s32[1,1,4]{2,1,0:T(1,128)} %bitcast.43), channel_id=1, replica_groups=mesh['row'=16,'col'=48] {'col'}, dimensions={0}, use_global_device_ids=true | all-gather | bytes 784 | tf_op jit(solution)/shard_map/all_gather | solution.py:15
  67.7 0.1 copy.38
  67.7 36.7 %all-gather.1 = s32[16,2,2]{2,1,0:T(2,128)S(1)} all-gather(s32[1,2,2]{2,1,0:T(2,128)} %bitcast.42), channel_id=1, replica_groups=mesh['row'=16,'col'=48] {'row'}, dimensions={0}, use_global_device_ids=true | all-gather | bytes 272 | tf_op jit(solution)/shard_map/all_gather | solution.py:12
  104.5 0.1 copy.46
  104.6 0.1 select_reduce_fusion
  104.7 0.1 copy.41
  104.8 0.1 reshape.21
  105.0 0.7 broadcast_compare_fusion.1
  105.7 0.1 copy.37
  105.8 0.1 fusion.25
  105.9 0.0 all-gather.5.cloned.1.call-done
  105.9 17.5 %gather_fusion = bf16[384,128,128]{2,1,0:T(8,128)(2,1)} fusion(bf16[32,2,128,128]{3,2,1,0:T(8,128)(2,1)} %all-gather.5.cloned.1.call-done, s32[384]{0:T(512)S(1)} %reshape.21), kind=kCustom, calls=%fused_computation | custom fusion | bytes 25168896 | tf_op jit(solution)/shard_map/gather | solution.py:22
  123.4 16.8 %copy.42 = bf16[4,48,2,128,128]{3,4,1,2,0:T(8,128)(2,1)} copy(bf16[4,48,2,128,128]{4,3,2,1,0:T(8,128)(2,1)} %bitcast.38) | data formatting | bytes 25165824 | tf_op jit(solution)/shard_map/gather | solution.py:22
  140.2 50.6 %all-gather.7.cloned.1.call-done = bf16[4,48,128,128]{3,2,1,0:T(8,128)(2,1)} async-done(((bf16[4,1,128,128]{3,2,1,0:T(8,128)(2,1)}), bf16[4,48,128,128]{3,2,1,0:T(8,128)(2,1)}) %all-gather.7.cloned.1.call-update) | async-done | bytes 6291472 | tf_op jit(solution)/shard_map/all_gather | solution.py:14
  190.8 8.3 %fusion.20 = bf16[4,2,128,128]{2,3,1,0:T(8,128)(2,1)S(1)} fusion(bf16[4,48,128,128]{3,2,1,0:T(8,128)(2,1)} %all-gather.7.cloned.1.call-done, bf16[4,48,2,128,128]{3,4,1,2,0:T(8,128)(2,1)} %copy.42, pred[4,48,2]{1,2,0:T(4,128)(4,1)S(1)} %fusion.25, pred[4,2]{1,0:T(4,128)(4,1)S(1)} %copy.37), kind=kOutput, calls=%fused_computation.9 | convolution fusion | flops 1617166336 | bytes 19136904 | tf_op jit(solution)/shard_map/inab,injbc->ijac/dot_general | solution.py:24
  199.1 0.8 copy.43
  (2 shorter events, 0.0 us)
Async XLA Ops:
  6.5 99.4 %all-gather.5.cloned.1.call-start = ((), (), s32[]{:S(2)}) async-start(), calls=%async_computation | async-start | bytes 2228224 | tf_op jit(solution)/shard_map/all_gather | solution.py:11
  7.3 183.5 %all-gather.7.cloned.1.call-start = ((), (), s32[]{:S(2)}) async-start(), calls=%async_computation.1 | async-start | bytes 6422528 | tf_op jit(solution)/shard_map/all_gather | solution.py:14
Sparse Core Ops, SparseCore 0:
  11.0 77.3 all-gather.4
  90.7 100.0 all-gather.6
where the time goes:
time: 207 us
  blocking collectives  96.4 us (47%)
  waiting for transfers between devices  52 us (25%)
  local copies, waits for them, and re-layouts  35.6 us (17%)
  between operations  13.4 us (6%)
  matrix products  8.33 us (4%)
    all_gather x1, blocking collectives, shards(): dense_cols = lax.all_gather(p_cols, 'col', axis=1, tiled=True)  59.7 us
    all_gather x1, waiting for transfers between devices, shards(): dense_blocks = lax.all_gather(p_blocks, 'col', axis=1, tiled=True)  50.6 us
    all_gather x1, blocking collectives, shards(): lax.all_gather(h_rows, 'row', axis=0, tiled=True)  36.7 us
    gather x2, local copies, waits for them, and re-layouts, shards(): picked = h_all[target, column_ids[None, None, :]]  34.3 us
    dot_general x1, matrix products, shards(): jnp.einsum('inab,injbc->ijac', dense_blocks, picked, preferred_element_ty...  8.33 us
  transfers between devices with their start and end apart: 2, of which 1 were waited for; matrix products, arithmetic and copies ran while one was open for 17% of the time, Pallas kernels for 0%

commit v1 on v0

v1 whole, which is shorter than its diff:
```python
import jax
import jax.numpy as jnp
from jax import lax
from jax.experimental import pallas as pl
from jax.experimental.pallas import tpu as pltpu
from jax.sharding import PartitionSpec as P

BS = 128
NX, NYH, NZ, NYL, NC = 4, 4, 12, 2, 2
ROWS = 4 * BS
META = 16
FULL = ROWS + META
SPLIT = 304
MESH = pl.DeviceIdType.MESH

ORDER = [
    ("M", 0), ("A", 0), ("F", -1), ("F", 1), ("H", -1, 0), ("H", 1, 0), ("H", 0, -1), ("H", 0, 1),
    ("B", 0), ("M", -1), ("M", 1), ("A", -1), ("A", 1), ("N", 0), ("B", -1), ("H", -2, 0),
    ("H", 1, -1), ("N", -1), ("B", 1), ("H", 0, -2), ("F", -2), ("F", 2), ("N", 1), ("A", -2),
    ("A", 2), ("M", -2), ("H", -1, -1), ("H", 1, 1), ("M", 2), ("B", -2), ("F", -3), ("F", 3),
    ("H", -1, 1), ("N", -2), ("B", 2), ("H", 1, -2), ("A", -3), ("A", 3), ("M", -3), ("M", 3),
    ("N", 2), ("B", -3), ("H", -1, -2), ("F", -4), ("F", 4), ("N", -3), ("B", 3), ("A", -4),
    ("A", 4), ("H", -2, -1), ("M", -4), ("M", 4), ("N", 3), ("B", -4), ("F", -5), ("F", 5),
    ("H", -2, 1), ("N", -4), ("B", 4), ("A", -5), ("A", 5), ("M", -5), ("M", 5), ("H", -2, -2),
    ("N", 4), ("C", 4), ("B", -5), ("F", -6), ("A", 6), ("N", -5), ("B", 5), ("M", -6), ("N", 5),
    ("C", 5), ("B", -6), ("N", -6), ("C", 6),
]
KINDS = {"F": 0, "A": 12, "B": 24, "M": 36, "N": 48}
SEMS = 76


def sem_index(event):
    if event[0] == "H":
        return 60 + (event[1] % 4) * 4 + event[2] % 4
    return KINDS[event[0]] + event[1] % 12


def kernel(p_ref, pc_ref, h_ref, hr_ref, keep_ref, out_ref, pbuf, hbuf, lhs, acc, send_sem, recv_sem, own_sem):
    row, col = lax.axis_index("row"), lax.axis_index("col")
    x, yh = row // NYH, row % NYH
    z, yl, core = col // 4, (col // 2) % 2, col % 2
    sign = 1 - 2 * core

    def col_of(dz, flip_pair, flip_core):
        zz = (z + sign * dz + 2 * NZ) % NZ
        return zz * 4 + (1 - yl if flip_pair else yl) * 2 + (1 - core if flip_core else core)

    def row_of(dx, dy):
        return ((x + sign * dx + 2 * NX) % NX) * NYH + (yh + sign * dy + 2 * NYH) % NYH

    links = {
        "zp": (row, col_of(1, False, False)),
        "zm": (row, col_of(-1, False, False)),
        "y": (row, col_of(0, True, False)),
        "m": (row, col_of(0, False, True)),
        "xp": (row_of(1, 0), col),
        "xm": (row_of(-1, 0), col),
        "hp": (row_of(0, 1), col),
        "hm": (row_of(0, -1), col),
    }

    def region(event):
        kind = event[0]
        if kind == "H":
            return hbuf.at[row_of(event[1], event[2])]
        d = event[1]
        if kind == "F":
            return pbuf.at[col_of(d, False, False)]
        if kind == "A":
            return pbuf.at[col_of(d, True, False), pl.ds(0, SPLIT)]
        if kind == "B":
            return pbuf.at[col_of(d, True, False), pl.ds(SPLIT, FULL - SPLIT)]
        if kind == "M":
            return pbuf.at[col_of(-d, False, True)]
        return pbuf.at[col_of(-d, True, True)]

    barrier = pltpu.get_barrier_semaphore()
    for device in links.values():
        pl.semaphore_signal(barrier, inc=1, device_id=device, device_id_type=MESH)

    own_p, own_h = pbuf.at[col], hbuf.at[row]
    copy_p = pltpu.make_async_copy(p_ref, pbuf.at[col, pl.ds(0, ROWS)], own_sem.at[0])
    copy_h = pltpu.make_async_copy(h_ref, hbuf.at[row, pl.ds(0, ROWS)], own_sem.at[1])
    copy_p.start()
    copy_h.start()
    line = lax.broadcasted_iota(jnp.int32, (META, BS), 0)
    p_meta = jnp.zeros((META, BS), jnp.int32)
    h_meta = jnp.zeros((META, BS), jnp.int32)
    base = 48 * (col // 3)
    for i in range(4):
        value = pc_ref[i, 0]
        p_meta = jnp.where(line // 4 == i, jnp.where(value < 0, -1, value - base), p_meta)
        value = hr_ref[i // 2, i % 2]
        h_meta = jnp.where(line % 4 == i, jnp.where(value < 0, -2, value - 48 * row), h_meta)
    pbuf[col, pl.ds(ROWS, META), :] = p_meta.astype(jnp.float32).astype(jnp.bfloat16)
    hbuf[row, pl.ds(ROWS, META), :] = h_meta.astype(jnp.float32).astype(jnp.bfloat16)
    copy_p.wait()
    copy_h.wait()
    pl.semaphore_wait(barrier, len(links))

    sent = []

    def send(link, source, event):
        copy = pltpu.make_async_remote_copy(
            src_ref=source,
            dst_ref=source,
            send_sem=send_sem.at[len(sent)],
            recv_sem=recv_sem.at[sem_index(event)],
            device_id=links[link],
            device_id_type=MESH,
        )
        copy.start()
        sent.append(copy)

    def receive(event):
        here = region(event)
        pltpu.make_async_remote_copy(
            src_ref=here,
            dst_ref=here,
            send_sem=send_sem.at[0],
            recv_sem=recv_sem.at[sem_index(event)],
            device_id=links["m"],
            device_id_type=MESH,
        ).wait_recv()
        return here

    first = pbuf.at[col, pl.ds(0, SPLIT)]
    second = pbuf.at[col, pl.ds(SPLIT, FULL - SPLIT)]
    send("y", first, ("A", 0))
    send("zp", own_p, ("F", -1))
    send("zm", own_p, ("F", 1))
    send("hp", own_h, ("H", 0, -1))
    send("hm", own_h, ("H", 0, 1))
    send("xp", own_h, ("H", -1, 0))
    send("xm", own_h, ("H", 1, 0))
    send("y", second, ("B", 0))
    send("m", own_p, ("M", 0))

    def block_row(step, carry):
        r = step % 16
        h_tags = hbuf[r, pl.ds(ROWS, META), :].astype(jnp.float32)
        tags = []
        for u in range(3):
            p_tags = pbuf[3 * r + u, pl.ds(ROWS, META), :].astype(jnp.float32)
            tags.append(jnp.where(p_tags == h_tags, 1.0, 0.0))
        for i in range(4):
            blocks = [pbuf[3 * r + u, pl.ds(i * BS, BS), :] for u in range(3)]
            for q in range(4):
                picked = None
                for u in range(3):
                    tag = jnp.broadcast_to(tags[u][4 * i + q : 4 * i + q + 1, :], (BS, BS))
                    term = blocks[u] * tag.astype(jnp.bfloat16)
                    picked = term if picked is None else picked + term
                lhs[q % 2, pl.ds(i * BS, BS), pl.ds((q // 2) * BS, BS)] = picked
        for j in range(2):
            rhs = jnp.concatenate(
                [hbuf[r, pl.ds(j * BS, BS), :], hbuf[r, pl.ds((2 + j) * BS, BS), :]], axis=0
            )
            acc[j] += jnp.dot(lhs[j], rhs, preferred_element_type=jnp.float32)
        return carry

    def low(s):
        return (4 * (z + NZ - s) + 2) // 3

    def high(s):
        return (4 * (z + NZ + s + 1)) // 3

    acc[...] = jnp.zeros_like(acc)
    done = None
    have = set()
    for event in ORDER:
        kind = event[0]
        if kind == "C":
            s = event[1]
            if s < 6:
                edges = (low(s), high(s))
            else:
                edges = (high(done[2]) - 16, low(done[2]) + 16)
            if done is None:
                lax.fori_loop(edges[0], edges[1], block_row, 0)
            elif s < 6:
                lax.fori_loop(edges[0], done[0], block_row, 0)
                lax.fori_loop(done[1], edges[1], block_row, 0)
            else:
                lax.fori_loop(done[1], done[0] + 16, block_row, 0)
            done = edges + (s,)
            continue
        here = receive(event)
        d = event[1]
        if kind == "F":
            if -6 < d < 0:
                send("zp", here, ("F", d - 1))
            if 0 < d < 5:
                send("zm", here, ("F", d + 1))
            place = col_of(d, False, False)
            send("y", pbuf.at[place, pl.ds(SPLIT, FULL - SPLIT)], ("B", d))
            send("m", here, ("M", d))
        elif kind in "AB":
            if kind == "A" and -5 < d <= 0:
                send("zp", here, ("A", d - 1))
            if kind == "A" and 0 <= d < 6:
                send("zm", here, ("A", d + 1))
            have.add((kind, d % 12))
            if ("A", d % 12) in have and ("B", d % 12) in have:
                send("m", pbuf.at[col_of(d, True, False)], ("N", d))
        elif kind == "H":
            dy = event[2]
            if d == 0:
                if dy == -1:
                    send("hp", here, ("H", 0, -2))
                send("xp", here, ("H", -1, dy))
                send("xm", here, ("H", 1, dy))
            elif d == -1:
                send("xp", here, ("H", -2, dy))

    for i in range(4):
        for j in range(2):
            total = acc[j, pl.ds(i * BS, BS), :]
            kept = jnp.where(keep_ref[i, j] == 1, total, jnp.zeros_like(total))
            out_ref[i, j] = kept.astype(out_ref.dtype)
    for copy in sent:
        copy.wait_send()


def shards(p_blocks, p_cols, h_blocks, h_rows, keep):
    smem = pl.BlockSpec(memory_space=pltpu.SMEM)
    anywhere = pl.BlockSpec(memory_space=pl.ANY)
    return pl.pallas_call(
        kernel,
        out_shape=jax.ShapeDtypeStruct((4, 2, BS, BS), jnp.bfloat16),
        in_specs=[anywhere, smem, anywhere, smem, smem],
        out_specs=pl.BlockSpec(memory_space=pltpu.VMEM),
        scratch_shapes=[
            pltpu.VMEM((NZ * 4, FULL, BS), jnp.bfloat16),
            pltpu.VMEM((NX * NYH, FULL, BS), jnp.bfloat16),
            pltpu.VMEM((2, ROWS, 2 * BS), jnp.bfloat16),
            pltpu.VMEM((2, ROWS, BS), jnp.float32),
            pltpu.SemaphoreType.DMA((SEMS,)),
            pltpu.SemaphoreType.DMA((SEMS,)),
            pltpu.SemaphoreType.DMA((2,)),
        ],
        compiler_params=pltpu.CompilerParams(
            collective_id=0, has_side_effects=True, vmem_limit_bytes=24 * 1024 * 1024
        ),
        name="filtered_product",
    )(p_blocks.reshape(ROWS, BS), p_cols, h_blocks.reshape(ROWS, BS), h_rows, keep)


def solution(mesh):
    return jax.shard_map(
        shards,
        mesh=mesh,
        in_specs=(
            P("row", "col", None, None),
            P("row", "col"),
            P("row", "col", None, None),
            P("row", "col"),
            P("row", "col"),
        ),
        out_specs=P("row", "col", None, None),
        check_vma=False,
    )
```

time: 207 us -> 67.1 us (0.32)
  blocking collectives: 96.4 us -> 0 us
  Pallas kernels: 0 us -> 62.4 us
  waiting for transfers between devices: 52 us -> 0 us
  local copies, waits for them, and re-layouts: 35.6 us -> 4.52 us
  between operations: 13.4 us -> 0.02 us
  matrix products: 8.33 us -> 0 us
    all_gather x2 -> x0, blocking collectives: 96.4 us -> none  [the longest x1 59.7 us: shards(): dense_cols = lax.all_gather(p_cols, 'col', axis=1, tiled=True)]
    pallas_call x0 -> x1, Pallas kernels: none -> 62.4 us  [shards(): pl.pallas_call(kernel, out_shape=jax.ShapeDtypeStruct((4, 2, BS, BS), jnp...]
    all_gather x2 -> x0, waiting for transfers between devices: 50.6 us -> none  [the longest x1 50.6 us: shards(): dense_blocks = lax.all_gather(p_blocks, 'col', axis=1, tiled=True)]
    gather x2 -> x0, local copies, waits for them, and re-layouts: 34.3 us -> none  [shards(): picked = h_all[target, column_ids[None, None, :]]]
    dot_general x1 -> x0, matrix products: 8.33 us -> none  [shards(): jnp.einsum('inab,injbc->ijac', dense_blocks, picked, preferred_element_ty...]
    unnamed x1 -> x13, local copies, waits for them, and re-layouts: 0.08 us -> 4.52 us
  transfers between devices with their start and end apart: 2 -> 0, of which waited for: 1 -> 0; matrix products, arithmetic and copies ran while one was open for 17% -> 0% of each run, Pallas kernels for 0% -> 0%
where the time goes in v1:
time: 67.1 us; the launch traced here: 66.9 us
  Pallas kernels  62.4 us (93%)
  local copies, waits for them, and re-layouts  4.52 us (7%)
    pallas_call x1, Pallas kernels, shards(): pl.pallas_call(kernel, out_shape=jax.ShapeDtypeStruct((4, 2, BS, BS), jnp...  62.4 us
    unnamed x13, local copies, waits for them, and re-layouts  4.52 us

profile of v1, /device:TPU:1, one launch (start us, length us, event | category | flops | bytes accessed | tf_op | source)
XLA Modules:
  0.0 66.9 jit_solution(6363942791347963893)
XLA Ops:
  0.0 0.0 copy-start.4
  0.0 0.7 copy-done.4
  0.7 0.0 copy-start.3
  0.7 0.1 copy.6.pc_ref
  0.8 0.6 copy-done.3
  1.3 0.0 copy-start.2
  1.3 0.1 copy.7.keep_ref
  1.4 0.6 copy-done.2
  2.0 0.0 copy-start
  2.0 0.9 %copy-done = bf16[4,1,128,128]{3,2,1,0:T(8,128)(2,1)S(1)} copy-done((bf16[4,1,128,128]{3,2,1,0:T(8,128)(2,1)S(1)}, bf16[4,1,128,128]{3,2,1,0:T(8,128)(2,1)}, u32[]{:S(2)}) %copy-start) | copy-done | bytes 131096
  2.9 0.0 copy-start.1
  2.9 0.9 %copy-done.1 = bf16[2,2,128,128]{3,2,1,0:T(8,128)(2,1)S(1)} copy-done((bf16[2,2,128,128]{3,2,1,0:T(8,128)(2,1)S(1)}, bf16[2,2,128,128]{3,2,1,0:T(8,128)(2,1)}, u32[]{:S(2)}) %copy-start.1) | copy-done | bytes 131096
  3.8 62.4 %filtered_product.1 = bf16[4,2,128,128]{3,2,1,0:T(8,128)(2,1)S(1)} custom-call(bf16[512,128]{1,0:T(8,128)(2,1)S(1)} %bitcast.2, s32[4,1]{1,0:T(4,128)S(1)} %copy.6.pc_ref, bf16[512,128]{1,0:T(8,128)(2,1)S(1)} %bitcast.3, s32[2,2]{1,0:T(2,128)S(1)} %copy-done.2, s32[4,2]{1,0:T(4,128)S(1)} %copy.7.keep_ref), custom_call_target="tpu_custom_call" | custom-call | tf_op jit(solution)/shard_map/filtered_product/pallas_call | solution.py:228
  66.2 0.7 %copy.9 = bf16[4,2,128,128]{3,2,1,0:T(8,128)(2,1)} copy(bf16[4,2,128,128]{3,2,1,0:T(8,128)(2,1)S(1)} %filtered_product.1) | data formatting | bytes 524288
Async XLA Ops:
  0.0 0.7 copy-start.4
  0.7 0.7 %copy-start.3 = (s32[4,2]{0,1:T(2,128)S(1)}, s32[4,2]{0,1:T(2,128)}, u32[]{:S(2)}) copy-start(s32[4,2]{0,1:T(2,128)} %param.9) | copy-start | bytes 100
  1.3 0.7 %copy-start.2 = (s32[2,2]{1,0:T(2,128)S(1)}, s32[2,2]{1,0:T(2,128)}, u32[]{:S(2)}) copy-start(s32[2,2]{1,0:T(2,128)} %hr_ref.1) | copy-start | bytes 52
  2.0 0.9 %copy-start = (bf16[4,1,128,128]{3,2,1,0:T(8,128)(2,1)S(1)}, bf16[4,1,128,128]{3,2,1,0:T(8,128)(2,1)}, u32[]{:S(2)}) copy-start(bf16[4,1,128,128]{3,2,1,0:T(8,128)(2,1)} %param.5) | copy-start | bytes 393220
  2.9 0.9 %copy-start.1 = (bf16[2,2,128,128]{3,2,1,0:T(8,128)(2,1)S(1)}, bf16[2,2,128,128]{3,2,1,0:T(8,128)(2,1)}, u32[]{:S(2)}) copy-start(bf16[2,2,128,128]{3,2,1,0:T(8,128)(2,1)} %param.7) | copy-start | bytes 393220

commit v2 on v1

v2 whole, which is shorter than its diff:
```python
import jax
import jax.numpy as jnp
from jax import lax
from jax.experimental import pallas as pl
from jax.experimental.pallas import tpu as pltpu
from jax.sharding import PartitionSpec as P

BS = 128
NX, NYH, NZ, NYL, NC = 4, 4, 12, 2, 2
ROWS = 4 * BS
META = 16
FULL = ROWS + META
SPLIT = 288
LAG = 41
MESH = pl.DeviceIdType.MESH

ORDER = [
    ("M", 0), ("E", -1), ("E", 1), ("A", 0), ("H", -1, 0), ("G", -1), ("G", 1), ("H", 1, 0), ("M", -1),
    ("E", -2), ("E", 2), ("M", 1), ("A", -1), ("H", 0, -1), ("H", -2, 0), ("A", 1), ("G", -2), ("G", 2),
    ("M", -2), ("E", -3), ("H", 0, 1), ("B", 0), ("E", 3), ("M", 2), ("H", -1, -1), ("A", -2), ("B", -1),
    ("N", 0), ("A", 2), ("H", 1, -1), ("G", -3), ("B", 1), ("N", -1), ("G", 3), ("H", -1, 1), ("M", -3),
    ("E", -4), ("B", -2), ("N", 1), ("E", 4), ("M", 3), ("H", 1, 1), ("B", 2), ("A", -3), ("N", -2), ("A", 3),
    ("H", -2, -1), ("N", 2), ("G", -4), ("G", 4), ("H", -2, 1), ("M", -4), ("E", -5), ("H", 0, -2), ("E", 5),
    ("M", 4), ("B", -3), ("A", -4), ("C", 2, 0), ("A", 4), ("B", 3), ("N", -3), ("G", -5), ("B", -4),
    ("G", 5), ("N", 3), ("H", -1, -2), ("M", -5), ("E", -6), ("B", 4), ("N", -4), ("A", -5), ("M", 5),
    ("H", 1, -2), ("A", 5), ("B", -5), ("N", 4), ("G", -6), ("C", 4, 1), ("B", 5), ("N", -5), ("H", -2, -2),
    ("M", -6), ("B", -6), ("A", 6), ("C", 4, 2), ("N", 5), ("N", 6), ("C", 6, 2),
]
FIRST = [
    ("y", ("A", 0)),
    ("zp", ("E", -1)),
    ("zm", ("E", 1)),
    ("zp", ("G", -1)),
    ("zm", ("G", 1)),
    ("hp", ("H", 0, -1)),
    ("hm", ("H", 0, 1)),
    ("xp", ("H", -1, 0)),
    ("xm", ("H", 1, 0)),
    ("y", ("B", 0)),
    ("m", ("M", 0)),
]
KINDS = {"E": 0, "A": 12, "B": 24, "M": 36, "N": 48, "G": 60}
SEMS = 88


def sem_index(event):
    if event[0] == "H":
        return 72 + (event[1] % 4) * 4 + event[2] % 4
    return KINDS[event[0]] + event[1] % 12


def kernel(
    p_ref, pc_hbm, h_ref, hr_hbm, keep_hbm, out_ref,
    pbuf, hbuf, lhs, acc, pc_ref, hr_ref, keep_ref, send_sem, recv_sem, own_sem,
):
    row, col = lax.axis_index("row"), lax.axis_index("col")
    x, yh = row // NYH, row % NYH
    z, yl, core = col // 4, (col // 2) % 2, col % 2
    sign = 1 - 2 * core

    def col_of(dz, flip_pair, flip_core):
        zz = (z + sign * dz + 2 * NZ) % NZ
        return zz * 4 + (1 - yl if flip_pair else yl) * 2 + (1 - core if flip_core else core)

    def row_of(dx, dy):
        return ((x + sign * dx + 2 * NX) % NX) * NYH + (yh + sign * dy + 2 * NYH) % NYH

    links = {
        "zp": (row, col_of(1, False, False)),
        "zm": (row, col_of(-1, False, False)),
        "y": (row, col_of(0, True, False)),
        "m": (row, col_of(0, False, True)),
        "xp": (row_of(1, 0), col),
        "xm": (row_of(-1, 0), col),
        "hp": (row_of(0, 1), col),
        "hm": (row_of(0, -1), col),
    }
    head, tail = pl.ds(0, SPLIT), pl.ds(SPLIT, FULL - SPLIT)

    def region(event):
        kind, d = event[0], event[1]
        if kind == "H":
            return hbuf.at[row_of(d, event[2])]
        if kind == "E":
            return pbuf.at[col_of(d, False, False), tail]
        if kind == "G":
            return pbuf.at[col_of(d, False, False), head]
        if kind == "A":
            return pbuf.at[col_of(d, True, False), head]
        if kind == "B":
            return pbuf.at[col_of(d, True, False), tail]
        if kind == "M":
            return pbuf.at[col_of(-d, False, True)]
        return pbuf.at[col_of(-d, True, True)]

    barrier = pltpu.get_barrier_semaphore()
    for device in links.values():
        pl.semaphore_signal(barrier, inc=1, device_id=device, device_id_type=MESH)

    own = [
        pltpu.make_async_copy(pc_hbm, pc_ref, own_sem.at[0]),
        pltpu.make_async_copy(hr_hbm, hr_ref, own_sem.at[1]),
        pltpu.make_async_copy(keep_hbm, keep_ref, own_sem.at[2]),
        pltpu.make_async_copy(p_ref, pbuf.at[col, pl.ds(0, ROWS)], own_sem.at[3]),
        pltpu.make_async_copy(h_ref, hbuf.at[row, pl.ds(0, ROWS)], own_sem.at[4]),
    ]
    for copy in own:
        copy.start()
    acc[...] = jnp.zeros_like(acc)
    own[0].wait()
    own[1].wait()
    line = lax.broadcasted_iota(jnp.int32, (META, BS), 0)
    p_meta = jnp.zeros((META, BS), jnp.int32)
    h_meta = jnp.zeros((META, BS), jnp.int32)
    base = 48 * (col // 3)
    for i in range(4):
        value = pc_ref[0, i]
        p_meta = jnp.where(line // 4 == i, jnp.where(value < 0, -1, value - base), p_meta)
        value = hr_ref[i // 2, i % 2]
        h_meta = jnp.where(line % 4 == i, jnp.where(value < 0, -2, value - 48 * row), h_meta)
    pbuf[col, pl.ds(ROWS, META), :] = p_meta.astype(jnp.float32).astype(jnp.bfloat16)
    hbuf[row, pl.ds(ROWS, META), :] = h_meta.astype(jnp.float32).astype(jnp.bfloat16)
    for copy in own[2:]:
        copy.wait()
    pl.semaphore_wait(barrier, len(links))

    sent = []

    def send(link, source, event):
        copy = pltpu.make_async_remote_copy(
            src_ref=source,
            dst_ref=source,
            send_sem=send_sem.at[len(sent)],
            recv_sem=recv_sem.at[sem_index(event)],
            device_id=links[link],
            device_id_type=MESH,
        )
        copy.start()
        sent.append(copy)

    def receive(event):
        here = region(event)
        pltpu.make_async_remote_copy(
            src_ref=here,
            dst_ref=here,
            send_sem=send_sem.at[0],
            recv_sem=recv_sem.at[sem_index(event)],
            device_id=links["m"],
            device_id_type=MESH,
        ).wait_recv()
        return here

    own_part = {"A": pbuf.at[col, head], "G": pbuf.at[col, head], "B": pbuf.at[col, tail], "E": pbuf.at[col, tail]}
    own_part.update({"M": pbuf.at[col], "H": hbuf.at[row]})
    for link, event in FIRST:
        send(link, own_part[event[0]], event)

    def block_row(r):
        h_tags = hbuf[r, pl.ds(ROWS, META), :].astype(jnp.float32)
        tags = []
        for u in range(3):
            p_tags = pbuf[3 * r + u, pl.ds(ROWS, META), :].astype(jnp.float32)
            tags.append(jnp.where(p_tags == h_tags, 1.0, 0.0))
        left = [[[None, None] for _ in range(4)] for _ in range(2)]
        for i in range(4):
            blocks = [pbuf[3 * r + u, pl.ds(i * BS, BS), :].reshape(8, META, BS) for u in range(3)]
            for q in range(4):
                picked = jnp.zeros_like(blocks[0])
                for u in range(3):
                    tag = jnp.broadcast_to(tags[u][4 * i + q : 4 * i + q + 1, :], (META, BS))
                    hit = jnp.broadcast_to(tag.astype(jnp.bfloat16)[None], (8, META, BS)) > 0
                    picked = jnp.where(hit, blocks[u], picked)
                left[q % 2][i][q // 2] = picked.reshape(BS, BS)
        right = [
            jnp.concatenate([hbuf[r, pl.ds(j * BS, BS), :], hbuf[r, pl.ds((2 + j) * BS, BS), :]], axis=0)
            for j in range(2)
        ]
        for m in range(2):
            sums = []
            for j in range(2):
                rows = jnp.concatenate([jnp.concatenate(v, axis=1) for v in left[j][2 * m : 2 * m + 2]], axis=0)
                sums.append(jnp.dot(rows, right[j], preferred_element_type=jnp.float32))
            for j in range(2):
                acc[j, pl.ds(m * 2 * BS, 2 * BS), :] += sums[j]

    def multiply(reach, before):
        def one(r, carry):
            dz = jnp.int32(0)
            for c in (3 * r, 3 * r + 2):
                d = (sign * (c // 4 - z) + NZ + 6) % NZ - 6
                dz = jnp.maximum(dz, jnp.maximum(d, -d))
            d = (r // NYH - x + NX) % NX
            dx = jnp.minimum(d, NX - d)
            now = (dz <= reach[0]) & (dx <= reach[1])
            if before is not None:
                now = now & ((dz > before[0]) | (dx > before[1]))
            pl.when(now)(lambda: block_row(r))
            return carry

        lax.fori_loop(0, NX * NYH, one, 0)

    reached = None
    have = set()
    retired = 0
    for event in ORDER:
        kind, d = event[0], event[1]
        if kind == "C":
            multiply(event[1:], reached)
            reached = event[1:]
            continue
        here = receive(event)
        have.add(event if kind == "H" else (kind, d % 12))
        if kind in "EGA":
            low, high = (-5, 6) if kind == "A" else (-6, 5)
            if low < d <= 0:
                send("zp", here, (kind, d - 1))
            if 0 <= d < high:
                send("zm", here, (kind, d + 1))
        if kind == "E":
            send("y", here, ("B", d))
        if kind in "EG" and ("E", d % 12) in have and ("G", d % 12) in have:
            send("m", pbuf.at[col_of(d, False, False)], ("M", d))
        if kind in "AB" and ("A", d % 12) in have and ("B", d % 12) in have:
            send("m", pbuf.at[col_of(d, True, False)], ("N", d))
        if kind == "H":
            dy = event[2]
            if d == 0:
                if dy == -1:
                    send("hp", here, ("H", 0, -2))
                send("xp", here, ("H", -1, dy))
                send("xm", here, ("H", 1, dy))
            elif d == -1:
                send("xp", here, ("H", -2, dy))
        while retired < len(sent) - LAG:
            sent[retired].wait_send()
            retired += 1

    for i in range(4):
        for j in range(2):
            total = acc[j, pl.ds(i * BS, BS), :]
            kept = jnp.where(keep_ref[j, i] == 1, total, jnp.zeros_like(total))
            out_ref[i, j] = kept.astype(out_ref.dtype)
    for copy in sent[retired:]:
        copy.wait_send()


def shards(p_blocks, p_cols, h_blocks, h_rows, keep):
    hbm = pl.BlockSpec(memory_space=pltpu.HBM)
    return pl.pallas_call(
        kernel,
        out_shape=jax.ShapeDtypeStruct((4, 2, BS, BS), jnp.bfloat16),
        in_specs=[hbm] * 5,
        out_specs=pl.BlockSpec(memory_space=pltpu.VMEM),
        scratch_shapes=[
            pltpu.VMEM((NZ * 4, FULL, BS), jnp.bfloat16),
            pltpu.VMEM((NX * NYH, FULL, BS), jnp.bfloat16),
            pltpu.VMEM((2, ROWS, 2 * BS), jnp.bfloat16),
            pltpu.VMEM((2, ROWS, BS), jnp.float32),
            pltpu.SMEM((1, 4), jnp.int32),
            pltpu.SMEM((2, 2), jnp.int32),
            pltpu.SMEM((2, 4), jnp.int32),
            pltpu.SemaphoreType.DMA((96,)),
            pltpu.SemaphoreType.DMA((SEMS,)),
            pltpu.SemaphoreType.DMA((5,)),
        ],
        compiler_params=pltpu.CompilerParams(
            collective_id=0, has_side_effects=True, vmem_limit_bytes=60 * 1024 * 1024
        ),
        name="filtered_product",
    )(p_blocks.reshape(ROWS, BS), p_cols.reshape(1, 4), h_blocks.reshape(ROWS, BS), h_rows, keep.T)


def solution(mesh):
    return jax.shard_map(
        shards,
        mesh=mesh,
        in_specs=(
            P("row", "col", None, None),
            P("row", "col"),
            P("row", "col", None, None),
            P("row", "col"),
            P("row", "col"),
        ),
        out_specs=P("row", "col", None, None),
        check_vma=False,
    )
```

time: 67.1 us -> 57.3 us (0.85)
  Pallas kernels: 62.4 us -> 55.4 us
  local copies, waits for them, and re-layouts: 4.52 us -> 1.67 us
    pallas_call x1, Pallas kernels: 62.4 us -> 55.4 us  [shards(): pl.pallas_call(kernel, out_shape=jax.ShapeDtypeStruct((4, 2, BS, BS), jnp...]
    unnamed x13 -> x1, local copies, waits for them, and re-layouts: 4.52 us -> 1.67 us
where the time goes in v2:
time: 57.3 us; the launch traced here: 57.1 us
  Pallas kernels  55.4 us (97%)
  local copies, waits for them, and re-layouts  1.67 us (3%)
    pallas_call x1, Pallas kernels, shards(): pl.pallas_call(kernel, out_shape=jax.ShapeDtypeStruct((4, 2, BS, BS), jnp...  55.4 us
    unnamed x1, local copies, waits for them, and re-layouts  1.67 us

profile of v2, /device:TPU:1, one launch (start us, length us, event | category | flops | bytes accessed | tf_op | source)
XLA Modules:
  0.0 57.1 jit_solution(16138240146771256207)
XLA Ops:
  0.0 55.4 %filtered_product.1 = bf16[4,2,128,128]{3,2,1,0:T(8,128)(2,1)} custom-call(bf16[512,128]{1,0:T(8,128)(2,1)} %bitcast.4, s32[1,4]{1,0:T(1,128)} %bitcast.7, bf16[512,128]{1,0:T(8,128)(2,1)} %bitcast.5, s32[2,2]{1,0:T(2,128)} %hr_hbm.1, s32[2,4]{1,0:T(2,128)} %bitcast.6), custom_call_target="tpu_custom_call" | custom-call | tf_op jit(solution)/shard_map/filtered_product/pallas_call | solution.py:249
  55.4 1.7 %copy.7 = bf16[4,2,128,128]{3,2,1,0:T(8,128)(2,1)} copy(bf16[4,2,128,128]{3,2,1,0:T(8,128)(2,1)} %filtered_product.1) | data formatting | bytes 524288

commit v3 on v2

--- a/solution.py
+++ b/solution.py
@@ -22,9 +22,9 @@
     ("E", -4), ("B", -2), ("N", 1), ("E", 4), ("M", 3), ("H", 1, 1), ("B", 2), ("A", -3), ("N", -2), ("A", 3),
     ("H", -2, -1), ("N", 2), ("G", -4), ("G", 4), ("H", -2, 1), ("M", -4), ("E", -5), ("H", 0, -2), ("E", 5),
     ("M", 4), ("B", -3), ("A", -4), ("C", 2, 0), ("A", 4), ("B", 3), ("N", -3), ("G", -5), ("B", -4),
-    ("G", 5), ("N", 3), ("H", -1, -2), ("M", -5), ("E", -6), ("B", 4), ("N", -4), ("A", -5), ("M", 5),
+    ("G", 5), ("N", 3), ("H", -1, -2), ("E", -6), ("M", -5), ("B", 4), ("N", -4), ("A", -5), ("M", 5),
     ("H", 1, -2), ("A", 5), ("B", -5), ("N", 4), ("G", -6), ("C", 4, 1), ("B", 5), ("N", -5), ("H", -2, -2),
-    ("M", -6), ("B", -6), ("A", 6), ("C", 4, 2), ("N", 5), ("N", 6), ("C", 6, 2),
+    ("M", -6), ("B", -6), ("A", 6), ("C", 4, 2), ("N", 5), ("C", 5, 2), ("N", 6), ("C", 6, 2),
 ]
 FIRST = [
     ("y", ("A", 0)),
@@ -58,12 +58,21 @@
     z, yl, core = col // 4, (col // 2) % 2, col % 2
     sign = 1 - 2 * core
 
+    def wrap(value, size):
+        value = jnp.where(value < 0, value + size, value)
+        return jnp.where(value >= size, value - size, value)
+
+    z_base = {dz: wrap(z + sign * dz, NZ) * 4 for dz in range(-6, 6)}
+    z_base[6] = z_base[-6]
+    in_chip = {(p, c): (1 - yl if p else yl) * 2 + (1 - core if c else core) for p in (0, 1) for c in (0, 1)}
+    x_base = {dx: wrap(x + sign * dx, NX) * NYH for dx in range(-2, 2)}
+    y_at = {dy: wrap(yh + sign * dy, NYH) for dy in range(-2, 2)}
+
     def col_of(dz, flip_pair, flip_core):
-        zz = (z + sign * dz + 2 * NZ) % NZ
-        return zz * 4 + (1 - yl if flip_pair else yl) * 2 + (1 - core if flip_core else core)
+        return z_base[dz] + in_chip[int(flip_pair), int(flip_core)]
 
     def row_of(dx, dy):
-        return ((x + sign * dx + 2 * NX) % NX) * NYH + (yh + sign * dy + 2 * NYH) % NYH
+        return x_base[dx] + y_at[dy]
 
     links = {
         "zp": (row, col_of(1, False, False)),
@@ -183,7 +192,20 @@
             for j in range(2):
                 acc[j, pl.ds(m * 2 * BS, 2 * BS), :] += sums[j]
 
+    def edges(s):
+        return (4 * (z + NZ - s) + 2) // 3, (4 * (z + NZ + s + 1)) // 3
+
     def multiply(reach, before):
+        if before is not None and before[1] == reach[1] == 2:
+            first, last = edges(reach[0]), edges(before[0])
+            if reach[0] == 6:
+                spans = [(last[1], last[0] + NX * NYH)]
+            else:
+                spans = [(first[0], last[0]), (last[1], first[1])]
+            for span in spans:
+                lax.fori_loop(span[0], span[1], lambda r, carry: block_row(r % (NX * NYH)) or carry, 0)
+            return
+
         def one(r, carry):
             dz = jnp.int32(0)
             for c in (3 * r, 3 * r + 2):
@@ -264,10 +286,13 @@
             pltpu.SemaphoreType.DMA((5,)),
         ],
         compiler_params=pltpu.CompilerParams(
-            collective_id=0, has_side_effects=True, vmem_limit_bytes=60 * 1024 * 1024
+            collective_id=0, has_side_effects=True, vmem_limit_bytes=24 * 1024 * 1024
         ),
         name="filtered_product",
-    )(p_blocks.reshape(ROWS, BS), p_cols.reshape(1, 4), h_blocks.reshape(ROWS, BS), h_rows, keep.T)
+    )(*[
+        pltpu.with_memory_space_constraint(array, pltpu.HBM)
+        for array in (p_blocks.reshape(ROWS, BS), p_cols.reshape(1, 4), h_blocks.reshape(ROWS, BS), h_rows, keep.T)
+    ])
 
 
 def solution(mesh):

time: 57.3 us -> 55.1 us (0.962)
  Pallas kernels: 55.4 us -> 54.3 us
  local copies, waits for them, and re-layouts: 1.67 us -> 0.71 us
    pallas_call x1, Pallas kernels: 55.4 us -> 54.3 us  [shards(): pl.pallas_call(kernel, out_shape=jax.ShapeDtypeStruct((4, 2, BS, BS), jnp...]
    unnamed x1, local copies, waits for them, and re-layouts: 1.67 us -> 0.71 us
where the time goes in v3:
time: 55.1 us; the launch traced here: 55 us
  Pallas kernels  54.3 us (99%)
  local copies, waits for them, and re-layouts  0.71 us (1%)
    pallas_call x1, Pallas kernels, shards(): pl.pallas_call(kernel, out_shape=jax.ShapeDtypeStruct((4, 2, BS, BS), jnp...  54.3 us

profile of v3, /device:TPU:1, one launch (start us, length us, event | category | flops | bytes accessed | tf_op | source)
XLA Modules:
  0.0 55.0 jit_solution(7275842670009257823)
XLA Ops:
  0.0 54.3 %filtered_product.1 = bf16[4,2,128,128]{3,2,1,0:T(8,128)(2,1)S(1)} custom-call(bf16[512,128]{1,0:T(8,128)(2,1)} %bitcast.4, s32[1,4]{1,0:T(1,128)} %bitcast.7, bf16[512,128]{1,0:T(8,128)(2,1)} %bitcast.5, s32[2,2]{1,0:T(2,128)} %hr_hbm.1, s32[2,4]{1,0:T(2,128)} %bitcast.6), custom_call_target="tpu_custom_call" | custom-call | tf_op jit(solution)/shard_map/filtered_product/pallas_call | solution.py:271
  54.3 0.7 %copy.7 = bf16[4,2,128,128]{3,2,1,0:T(8,128)(2,1)} copy(bf16[4,2,128,128]{3,2,1,0:T(8,128)(2,1)S(1)} %filtered_product.1) | data formatting | bytes 524288

commit v4 on v3

--- a/solution.py
+++ b/solution.py
@@ -11,7 +11,9 @@
 META = 16
 FULL = ROWS + META
 SPLIT = 288
+NEAR = 6
 LAG = 41
+LAST_LAG = 12
 MESH = pl.DeviceIdType.MESH
 
 ORDER = [
@@ -110,11 +112,41 @@
         pltpu.make_async_copy(pc_hbm, pc_ref, own_sem.at[0]),
         pltpu.make_async_copy(hr_hbm, hr_ref, own_sem.at[1]),
         pltpu.make_async_copy(keep_hbm, keep_ref, own_sem.at[2]),
-        pltpu.make_async_copy(p_ref, pbuf.at[col, pl.ds(0, ROWS)], own_sem.at[3]),
-        pltpu.make_async_copy(h_ref, hbuf.at[row, pl.ds(0, ROWS)], own_sem.at[4]),
+        pltpu.make_async_copy(p_ref, pbuf.at[col, pl.ds(META, ROWS)], own_sem.at[3]),
+        pltpu.make_async_copy(h_ref, hbuf.at[row, pl.ds(META, ROWS)], own_sem.at[4]),
     ]
     for copy in own:
         copy.start()
+    sent = []
+
+    def send(link, source, event):
+        copy = pltpu.make_async_remote_copy(
+            src_ref=source,
+            dst_ref=region(("E", 0)) if event in (("E", 1), ("E", -1)) else source,
+            send_sem=send_sem.at[len(sent)],
+            recv_sem=recv_sem.at[sem_index(event)],
+            device_id=links[link],
+            device_id_type=MESH,
+        )
+        copy.start()
+        sent.append(copy)
+
+    def receive(event):
+        here = region(event)
+        pltpu.make_async_remote_copy(
+            src_ref=here,
+            dst_ref=here,
+            send_sem=send_sem.at[0],
+            recv_sem=recv_sem.at[sem_index(event)],
+            device_id=links["m"],
+            device_id_type=MESH,
+        ).wait_recv()
+        return here
+
+    pl.semaphore_wait(barrier, len(links))
+    rest = p_ref.at[pl.ds(SPLIT - META, FULL - SPLIT)]
+    send("zp", rest, ("E", -1))
+    send("zm", rest, ("E", 1))
     acc[...] = jnp.zeros_like(acc)
     own[0].wait()
     own[1].wait()
@@ -127,52 +159,25 @@
         p_meta = jnp.where(line // 4 == i, jnp.where(value < 0, -1, value - base), p_meta)
         value = hr_ref[i // 2, i % 2]
         h_meta = jnp.where(line % 4 == i, jnp.where(value < 0, -2, value - 48 * row), h_meta)
-    pbuf[col, pl.ds(ROWS, META), :] = p_meta.astype(jnp.float32).astype(jnp.bfloat16)
-    hbuf[row, pl.ds(ROWS, META), :] = h_meta.astype(jnp.float32).astype(jnp.bfloat16)
+    pbuf[col, pl.ds(0, META), :] = p_meta.astype(jnp.float32).astype(jnp.bfloat16)
+    hbuf[row, pl.ds(0, META), :] = h_meta.astype(jnp.float32).astype(jnp.bfloat16)
     for copy in own[2:]:
         copy.wait()
-    pl.semaphore_wait(barrier, len(links))
-
-    sent = []
-
-    def send(link, source, event):
-        copy = pltpu.make_async_remote_copy(
-            src_ref=source,
-            dst_ref=source,
-            send_sem=send_sem.at[len(sent)],
-            recv_sem=recv_sem.at[sem_index(event)],
-            device_id=links[link],
-            device_id_type=MESH,
-        )
-        copy.start()
-        sent.append(copy)
-
-    def receive(event):
-        here = region(event)
-        pltpu.make_async_remote_copy(
-            src_ref=here,
-            dst_ref=here,
-            send_sem=send_sem.at[0],
-            recv_sem=recv_sem.at[sem_index(event)],
-            device_id=links["m"],
-            device_id_type=MESH,
-        ).wait_recv()
-        return here
-
-    own_part = {"A": pbuf.at[col, head], "G": pbuf.at[col, head], "B": pbuf.at[col, tail], "E": pbuf.at[col, tail]}
+    own_part = {"A": pbuf.at[col, head], "G": pbuf.at[col, head], "B": pbuf.at[col, tail]}
     own_part.update({"M": pbuf.at[col], "H": hbuf.at[row]})
     for link, event in FIRST:
-        send(link, own_part[event[0]], event)
+        if event[0] != "E":
+            send(link, own_part[event[0]], event)
 
     def block_row(r):
-        h_tags = hbuf[r, pl.ds(ROWS, META), :].astype(jnp.float32)
+        h_tags = hbuf[r, pl.ds(0, META), :].astype(jnp.float32)
         tags = []
         for u in range(3):
-            p_tags = pbuf[3 * r + u, pl.ds(ROWS, META), :].astype(jnp.float32)
+            p_tags = pbuf[3 * r + u, pl.ds(0, META), :].astype(jnp.float32)
             tags.append(jnp.where(p_tags == h_tags, 1.0, 0.0))
         left = [[[None, None] for _ in range(4)] for _ in range(2)]
         for i in range(4):
-            blocks = [pbuf[3 * r + u, pl.ds(i * BS, BS), :].reshape(8, META, BS) for u in range(3)]
+            blocks = [pbuf[3 * r + u, pl.ds(META + i * BS, BS), :].reshape(8, META, BS) for u in range(3)]
             for q in range(4):
                 picked = jnp.zeros_like(blocks[0])
                 for u in range(3):
@@ -181,7 +186,7 @@
                     picked = jnp.where(hit, blocks[u], picked)
                 left[q % 2][i][q // 2] = picked.reshape(BS, BS)
         right = [
-            jnp.concatenate([hbuf[r, pl.ds(j * BS, BS), :], hbuf[r, pl.ds((2 + j) * BS, BS), :]], axis=0)
+            jnp.concatenate([hbuf[r, pl.ds(META + j * BS, BS), :], hbuf[r, pl.ds(META + (2 + j) * BS, BS), :]], axis=0)
             for j in range(2)
         ]
         for m in range(2):
@@ -224,7 +229,7 @@
     reached = None
     have = set()
     retired = 0
-    for event in ORDER:
+    for place, event in enumerate(ORDER):
         kind, d = event[0], event[1]
         if kind == "C":
             multiply(event[1:], reached)
@@ -238,8 +243,12 @@
                 send("zp", here, (kind, d - 1))
             if 0 <= d < high:
                 send("zm", here, (kind, d + 1))
-        if kind == "E":
+        if kind == "E" and abs(d) <= NEAR:
             send("y", here, ("B", d))
+        if kind == "B" and -5 < d <= -NEAR:
+            send("zp", here, ("B", d - 1))
+        if kind == "B" and NEAR <= d < 6:
+            send("zm", here, ("B", d + 1))
         if kind in "EG" and ("E", d % 12) in have and ("G", d % 12) in have:
             send("m", pbuf.at[col_of(d, False, False)], ("M", d))
         if kind in "AB" and ("A", d % 12) in have and ("B", d % 12) in have:
@@ -253,7 +262,8 @@
                 send("xm", here, ("H", 1, dy))
             elif d == -1:
                 send("xp", here, ("H", -2, dy))
-        while retired < len(sent) - LAG:
+        lag = LAG if place < len(ORDER) - 8 else LAST_LAG
+        while retired < len(sent) - lag:
             sent[retired].wait_send()
             retired += 1
 

time: 55.1 us -> 55.1 us (level)
  no operation moved by 1% of the time
where the time goes in v4:
time: 55.1 us; the launch traced here: 55 us
  Pallas kernels  54.3 us (99%)
  local copies, waits for them, and re-layouts  0.71 us (1%)
    pallas_call x1, Pallas kernels, shards(): pl.pallas_call(kernel, out_shape=jax.ShapeDtypeStruct((4, 2, BS, BS), jnp...  54.3 us

profile of v4, /device:TPU:1, one launch (start us, length us, event | category | flops | bytes accessed | tf_op | source)
XLA Modules:
  0.0 55.0 jit_solution(14806620572463380847)
XLA Ops:
  0.0 54.3 %filtered_product.1 = bf16[4,2,128,128]{3,2,1,0:T(8,128)(2,1)S(1)} custom-call(bf16[512,128]{1,0:T(8,128)(2,1)} %bitcast.4, s32[1,4]{1,0:T(1,128)} %bitcast.7, bf16[512,128]{1,0:T(8,128)(2,1)} %bitcast.5, s32[2,2]{1,0:T(2,128)} %hr_hbm.1, s32[2,4]{1,0:T(2,128)} %bitcast.6), custom_call_target="tpu_custom_call" | custom-call | tf_op jit(solution)/shard_map/filtered_product/pallas_call | solution.py:281
  54.3 0.7 %copy.7 = bf16[4,2,128,128]{3,2,1,0:T(8,128)(2,1)} copy(bf16[4,2,128,128]{3,2,1,0:T(8,128)(2,1)S(1)} %filtered_product.1) | data formatting | bytes 524288

commit v5 on v3

--- a/solution.py
+++ b/solution.py
@@ -10,21 +10,22 @@
 ROWS = 4 * BS
 META = 16
 FULL = ROWS + META
-SPLIT = 288
-LAG = 41
+SPLIT = 256
+LAG = 42
 MESH = pl.DeviceIdType.MESH
 
 ORDER = [
-    ("M", 0), ("E", -1), ("E", 1), ("A", 0), ("H", -1, 0), ("G", -1), ("G", 1), ("H", 1, 0), ("M", -1),
-    ("E", -2), ("E", 2), ("M", 1), ("A", -1), ("H", 0, -1), ("H", -2, 0), ("A", 1), ("G", -2), ("G", 2),
-    ("M", -2), ("E", -3), ("H", 0, 1), ("B", 0), ("E", 3), ("M", 2), ("H", -1, -1), ("A", -2), ("B", -1),
-    ("N", 0), ("A", 2), ("H", 1, -1), ("G", -3), ("B", 1), ("N", -1), ("G", 3), ("H", -1, 1), ("M", -3),
-    ("E", -4), ("B", -2), ("N", 1), ("E", 4), ("M", 3), ("H", 1, 1), ("B", 2), ("A", -3), ("N", -2), ("A", 3),
-    ("H", -2, -1), ("N", 2), ("G", -4), ("G", 4), ("H", -2, 1), ("M", -4), ("E", -5), ("H", 0, -2), ("E", 5),
-    ("M", 4), ("B", -3), ("A", -4), ("C", 2, 0), ("A", 4), ("B", 3), ("N", -3), ("G", -5), ("B", -4),
-    ("G", 5), ("N", 3), ("H", -1, -2), ("E", -6), ("M", -5), ("B", 4), ("N", -4), ("A", -5), ("M", 5),
-    ("H", 1, -2), ("A", 5), ("B", -5), ("N", 4), ("G", -6), ("C", 4, 1), ("B", 5), ("N", -5), ("H", -2, -2),
-    ("M", -6), ("B", -6), ("A", 6), ("C", 4, 2), ("N", 5), ("C", 5, 2), ("N", 6), ("C", 6, 2),
+    ("M", 0), ("E", -1), ("A", 0), ("E", 1), ("H", -1, 0), ("G", -1), ("G", 1), ("H", 1, 0), ("M", -1),
+    ("E", -2), ("M", 1), ("A", -1), ("H", 0, -1), ("A", 1), ("H", -2, 0), ("E", 2), ("G", -2), ("G", 2),
+    ("H", 0, 1), ("M", -2), ("E", -3), ("B", 0), ("M", 2), ("A", -2), ("H", -1, -1), ("A", 2), ("N", 0),
+    ("B", -1), ("E", 3), ("H", 1, -1), ("G", -3), ("N", -1), ("G", 3), ("B", 1), ("H", -1, 1), ("M", -3),
+    ("E", -4), ("A", -3), ("M", 3), ("H", 1, 1), ("B", -2), ("N", 1), ("A", 3), ("E", 4), ("H", -2, -1),
+    ("N", -2), ("G", -4), ("G", 4), ("H", -2, 1), ("M", -4), ("E", -5), ("H", 0, -2), ("M", 4), ("A", -4),
+    ("B", 2), ("A", 4), ("C", 1, 0), ("E", 5), ("N", 2), ("B", -3), ("G", -5), ("C", 2, 0), ("G", 5),
+    ("B", 3), ("N", -3), ("H", -1, -2), ("M", -5), ("E", -6), ("A", -5), ("M", 5), ("N", 3), ("B", -4),
+    ("H", 1, -2), ("A", 5), ("C", 3, 1), ("G", -6), ("N", -4), ("B", 4), ("H", -2, -2), ("B", -5), ("A", 6),
+    ("C", 3, 2), ("M", -6), ("B", 5), ("N", 4), ("N", -5), ("C", 4, 2), ("B", -6), ("N", 5), ("C", 5, 2),
+    ("N", -6), ("C", 6, 2),
 ]
 FIRST = [
     ("y", ("A", 0)),

time: 55.1 us -> 54.6 us (level)
  no operation moved by 1% of the time
where the time goes in v5:
time: 54.6 us; the launch traced here: 54.5 us
  Pallas kernels  53.8 us (99%)
  local copies, waits for them, and re-layouts  0.71 us (1%)
    pallas_call x1, Pallas kernels, shards(): pl.pallas_call(kernel, out_shape=jax.ShapeDtypeStruct((4, 2, BS, BS), jnp...  53.8 us

profile of v5, /device:TPU:1, one launch (start us, length us, event | category | flops | bytes accessed | tf_op | source)
XLA Modules:
  0.0 54.5 jit_solution(1847696884048084583)
XLA Ops:
  0.0 53.8 %filtered_product.1 = bf16[4,2,128,128]{3,2,1,0:T(8,128)(2,1)S(1)} custom-call(bf16[512,128]{1,0:T(8,128)(2,1)} %bitcast.4, s32[1,4]{1,0:T(1,128)} %bitcast.7, bf16[512,128]{1,0:T(8,128)(2,1)} %bitcast.5, s32[2,2]{1,0:T(2,128)} %hr_hbm.1, s32[2,4]{1,0:T(2,128)} %bitcast.6), custom_call_target="tpu_custom_call" | custom-call | tf_op jit(solution)/shard_map/filtered_product/pallas_call | solution.py:272
  53.8 0.7 %copy.7 = bf16[4,2,128,128]{3,2,1,0:T(8,128)(2,1)} copy(bf16[4,2,128,128]{3,2,1,0:T(8,128)(2,1)S(1)} %filtered_product.1) | data formatting | bytes 524288

commit v6 on v5

--- a/solution.py
+++ b/solution.py
@@ -21,7 +21,7 @@
     ("B", -1), ("E", 3), ("H", 1, -1), ("G", -3), ("N", -1), ("G", 3), ("B", 1), ("H", -1, 1), ("M", -3),
     ("E", -4), ("A", -3), ("M", 3), ("H", 1, 1), ("B", -2), ("N", 1), ("A", 3), ("E", 4), ("H", -2, -1),
     ("N", -2), ("G", -4), ("G", 4), ("H", -2, 1), ("M", -4), ("E", -5), ("H", 0, -2), ("M", 4), ("A", -4),
-    ("B", 2), ("A", 4), ("C", 1, 0), ("E", 5), ("N", 2), ("B", -3), ("G", -5), ("C", 2, 0), ("G", 5),
+    ("B", 2), ("A", 4), ("E", 5), ("N", 2), ("B", -3), ("G", -5), ("C", 2, 0), ("G", 5),
     ("B", 3), ("N", -3), ("H", -1, -2), ("M", -5), ("E", -6), ("A", -5), ("M", 5), ("N", 3), ("B", -4),
     ("H", 1, -2), ("A", 5), ("C", 3, 1), ("G", -6), ("N", -4), ("B", 4), ("H", -2, -2), ("B", -5), ("A", 6),
     ("C", 3, 2), ("M", -6), ("B", 5), ("N", 4), ("N", -5), ("C", 4, 2), ("B", -6), ("N", 5), ("C", 5, 2),

time: 54.6 us -> 54.6 us (level)
  no operation moved by 1% of the time
where the time goes in v6:
time: 54.6 us; the launch traced here: 54.5 us
  Pallas kernels  53.8 us (99%)
  local copies, waits for them, and re-layouts  0.71 us (1%)
    pallas_call x1, Pallas kernels, shards(): pl.pallas_call(kernel, out_shape=jax.ShapeDtypeStruct((4, 2, BS, BS), jnp...  53.8 us

profile of v6, /device:TPU:1, one launch (start us, length us, event | category | flops | bytes accessed | tf_op | source)
XLA Modules:
  0.0 54.5 jit_solution(18212854890836578876)
XLA Ops:
  0.0 53.8 %filtered_product.1 = bf16[4,2,128,128]{3,2,1,0:T(8,128)(2,1)S(1)} custom-call(bf16[512,128]{1,0:T(8,128)(2,1)} %bitcast.4, s32[1,4]{1,0:T(1,128)} %bitcast.7, bf16[512,128]{1,0:T(8,128)(2,1)} %bitcast.5, s32[2,2]{1,0:T(2,128)} %hr_hbm.1, s32[2,4]{1,0:T(2,128)} %bitcast.6), custom_call_target="tpu_custom_call" | custom-call | tf_op jit(solution)/shard_map/filtered_product/pallas_call | solution.py:272
  53.8 0.7 %copy.7 = bf16[4,2,128,128]{3,2,1,0:T(8,128)(2,1)} copy(bf16[4,2,128,128]{3,2,1,0:T(8,128)(2,1)S(1)} %filtered_product.1) | data formatting | bytes 524288

commit v7 on v5

--- a/solution.py
+++ b/solution.py
@@ -225,7 +225,7 @@
     reached = None
     have = set()
     retired = 0
-    for event in ORDER:
+    for place, event in enumerate(ORDER):
         kind, d = event[0], event[1]
         if kind == "C":
             multiply(event[1:], reached)
@@ -254,7 +254,7 @@
                 send("xm", here, ("H", 1, dy))
             elif d == -1:
                 send("xp", here, ("H", -2, dy))
-        while retired < len(sent) - LAG:
+        while retired < len(sent) - (LAG if place < len(ORDER) - 8 else 12):
             sent[retired].wait_send()
             retired += 1
 

time: 54.6 us -> 54.6 us (level)
  no operation moved by 1% of the time
where the time goes in v7:
time: 54.6 us; the launch traced here: 54.4 us
  Pallas kernels  53.7 us (98%)
  local copies, waits for them, and re-layouts  0.71 us (1%)
    pallas_call x1, Pallas kernels, shards(): pl.pallas_call(kernel, out_shape=jax.ShapeDtypeStruct((4, 2, BS, BS), jnp...  53.7 us

profile of v7, /device:TPU:1, one launch (start us, length us, event | category | flops | bytes accessed | tf_op | source)
XLA Modules:
  0.0 54.4 jit_solution(14078098225474669083)
XLA Ops:
  0.0 53.7 %filtered_product.1 = bf16[4,2,128,128]{3,2,1,0:T(8,128)(2,1)S(1)} custom-call(bf16[512,128]{1,0:T(8,128)(2,1)} %bitcast.4, s32[1,4]{1,0:T(1,128)} %bitcast.7, bf16[512,128]{1,0:T(8,128)(2,1)} %bitcast.5, s32[2,2]{1,0:T(2,128)} %hr_hbm.1, s32[2,4]{1,0:T(2,128)} %bitcast.6), custom_call_target="tpu_custom_call" | custom-call | tf_op jit(solution)/shard_map/filtered_product/pallas_call | solution.py:272
  53.7 0.7 %copy.7 = bf16[4,2,128,128]{3,2,1,0:T(8,128)(2,1)} copy(bf16[4,2,128,128]{3,2,1,0:T(8,128)(2,1)S(1)} %filtered_product.1) | data formatting | bytes 524288
